TPU v7x, 256 devices: a whole 4x4x8 slice. The times are simulated.
256 devices in a mesh: segment: 16 (over x_hi, y, core), expert: 16 (over x_lo, z).
Axes of the slice: x: 4 (x_hi: 2, x_lo: 2; x = x_hi * 2 + x_lo), y: 4, z: 8, core: 2. Of those that a mesh axis runs over, the one named last changes fastest.
Arguments:
- fwd_tokens: bfloat16 [16, 2048, 2048], P('segment', 'expert'), may hold values from -6 to 6
- fwd_routes: int32 [16, 2048, 2], P('segment', 'expert'), may hold values from 0 to 15, all different within a row; in each aligned block of 128 rows (0 to 127, 128 to 255, ..., all dimensions but the last counted through in order) at most 32 rows name the same one
- fwd_weights: float32 [16, 2048, 2], P('segment', 'expert'), may hold values from 0.2 to 1
- saved_tokens: bfloat16 [16, 2048, 2048], P('segment', 'expert'), may hold values from -6 to 6
- bwd_routes: int32 [16, 2048, 2], P('segment', 'expert'), may hold values from 0 to 15, all different within a row; in each aligned block of 128 rows (0 to 127, 128 to 255, ..., all dimensions but the last counted through in order) at most 32 rows name the same one
- bwd_weights: float32 [16, 2048, 2], P('segment', 'expert'), may hold values from 0.2 to 1
- incoming_grad: bfloat16 [16, 2048, 2048], P('segment', 'expert'), may hold values from -6 to 6
- norm_gain: float32 [16, 2048], P('segment'), may hold values from 0.1 to 1.9
- gate_proj: bfloat16 [16, 16, 2048, 768], P('segment', 'expert'), may hold values from -0.125 to 0.125
- up_proj: bfloat16 [16, 16, 2048, 768], P('segment', 'expert'), may hold values from -0.125 to 0.125
- down_proj: bfloat16 [16, 16, 768, 2048], P('segment', 'expert'), may hold values from -0.21875 to 0.21875
Outputs:
- next_input: bfloat16 [16, 2048, 2048], P('segment', 'expert')
- next_grad: bfloat16 [16, 2048, 2048], P('segment', 'expert')
- combine_grad: bfloat16 [16, 2048, 2], P('segment', 'expert')
Inputs may be any that keep to these rules, and one draw needn't show every extreme that they name: `fwd_routes`: each token names 2 different experts. In each aligned block of 128 rows of a section (the rows of one device), no expert is named more than 32 times, and in every draw some expert is named exactly 32 times in some block. `bwd_routes`: as for fwd_routes.
All inputs are finite; a program needn't handle non-finite values.
Results may differ from a plain program's by a relative error of at most 0.012.
Values may be sent and summed in bfloat16 or wider, within the bound.
A program may use at most 128 MiB of HBM per device.

v0:
```python
import jax
import jax.numpy as jnp
from jax import lax
from jax.sharding import PartitionSpec as P

EPS = 1e-06


def from_behind(value, axis, steps):
    count = lax.axis_size(axis)
    pairs = [(source, (source + steps) % count) for source in range(count)]
    return lax.ppermute(value, axis, pairs)


def slot_index(route_block, expert_count, capacity):
    flat_route = route_block.reshape(-1)
    chosen = (flat_route[:, None] == jnp.arange(expert_count, dtype=jnp.int32)[None, :]).astype(
        jnp.int32
    )
    before = jnp.cumsum(chosen, axis=0) - chosen
    return flat_route * capacity + jnp.sum(before * chosen, axis=1)


def pack_rows(token_rows, slot_rows, expert_count, capacity):
    top_count = slot_rows.shape[0] // token_rows.shape[0]
    spread = jnp.repeat(token_rows, top_count, axis=0)
    packed = (
        jnp.zeros((expert_count * capacity, token_rows.shape[1]), token_rows.dtype)
        .at[slot_rows]
        .set(spread)
    )
    return packed.reshape(expert_count, capacity, token_rows.shape[1])


def unpack_rows(packed, slot_rows, top_count):
    flat_rows = packed.reshape((-1,) + packed.shape[2:])
    picked = flat_rows[slot_rows]
    return picked.reshape((slot_rows.shape[0] // top_count, top_count) + packed.shape[2:])


def dot_rows(left_rows, right_matrix):
    return jnp.dot(left_rows, right_matrix, preferred_element_type=jnp.float32)


def dot_back(left_rows, right_matrix):
    return lax.dot_general(
        left_rows, right_matrix, (((1,), (1,)), ((), ())), preferred_element_type=jnp.float32
    )


def normalize(token_rows, gain_row):
    values = token_rows.astype(jnp.float32)
    inv_scale = lax.rsqrt(jnp.mean(values * values, axis=-1, keepdims=True) + EPS)
    return (values * inv_scale * gain_row, inv_scale)


def expert_forward(token_rows, w_gate, w_up, w_down):
    gate_pre = dot_rows(token_rows, w_gate)
    up_pre = dot_rows(token_rows, w_up)
    hidden = (gate_pre * jax.nn.sigmoid(gate_pre) * up_pre).astype(jnp.bfloat16)
    return dot_rows(hidden, w_down).astype(jnp.bfloat16)


def expert_backward(token_rows, grad_rows, w_gate, w_up, w_down):
    gate_pre = dot_rows(token_rows, w_gate)
    up_pre = dot_rows(token_rows, w_up)
    sigmoid = jax.nn.sigmoid(gate_pre)
    active = gate_pre * sigmoid
    hidden = (active * up_pre).astype(jnp.bfloat16)
    output = dot_rows(hidden, w_down).astype(jnp.bfloat16)
    weight_grad = jnp.sum(
        output.astype(jnp.float32) * grad_rows.astype(jnp.float32), axis=1
    ).astype(jnp.bfloat16)
    hidden_grad = dot_back(grad_rows, w_down)
    gate_grad = (hidden_grad * up_pre * sigmoid * (1.0 + gate_pre * (1.0 - sigmoid))).astype(
        jnp.bfloat16
    )
    up_grad = (hidden_grad * active).astype(jnp.bfloat16)
    row_grad = (dot_back(gate_grad, w_gate) + dot_back(up_grad, w_up)).astype(jnp.bfloat16)
    return (row_grad, weight_grad)


def body(
    fwd_tokens,
    fwd_routes,
    fwd_weights,
    saved_tokens,
    bwd_routes,
    bwd_weights,
    incoming_grad,
    norm_gain,
    gate_proj,
    up_proj,
    down_proj,
):
    expert_count = lax.axis_size("expert")
    fwd_rows = fwd_tokens[0]
    token_count = fwd_rows.shape[0]
    feature_width = fwd_rows.shape[1]
    top_count = fwd_routes.shape[2]
    capacity = 2 * token_count * top_count // expert_count
    gain_row = norm_gain[0]
    w_gate = gate_proj[0, 0]
    w_up = up_proj[0, 0]
    w_down = down_proj[0, 0]
    fwd_index = slot_index(fwd_routes[0], expert_count, capacity)
    bwd_index = slot_index(bwd_routes[0], expert_count, capacity)
    normed_fwd, fwd_scale = normalize(fwd_rows, gain_row)
    fwd_send = pack_rows(normed_fwd.astype(jnp.bfloat16), fwd_index, expert_count, capacity)
    bwd_rows = saved_tokens[0]
    grad_rows = incoming_grad[0]
    normed_saved, saved_scale = normalize(bwd_rows, gain_row)
    saved_send = pack_rows(normed_saved.astype(jnp.bfloat16), bwd_index, expert_count, capacity)
    grad_send = pack_rows(grad_rows, bwd_index, expert_count, capacity)
    fwd_in = lax.all_to_all(fwd_send, "expert", split_axis=0, concat_axis=0, tiled=True)
    saved_in = lax.all_to_all(saved_send, "expert", split_axis=0, concat_axis=0, tiled=True)
    grad_in = lax.all_to_all(grad_send, "expert", split_axis=0, concat_axis=0, tiled=True)
    source_count = fwd_in.shape[0]
    slot_count = fwd_in.shape[1]
    flat_count = source_count * slot_count
    fwd_out = expert_forward(fwd_in.reshape(flat_count, feature_width), w_gate, w_up, w_down)
    row_grad, weight_grad = expert_backward(
        saved_in.reshape(flat_count, feature_width),
        grad_in.reshape(flat_count, feature_width),
        w_gate,
        w_up,
        w_down,
    )
    fwd_back = lax.all_to_all(
        fwd_out.reshape(source_count, slot_count, feature_width),
        "expert",
        split_axis=0,
        concat_axis=0,
        tiled=True,
    )
    grad_back = lax.all_to_all(
        row_grad.reshape(source_count, slot_count, feature_width),
        "expert",
        split_axis=0,
        concat_axis=0,
        tiled=True,
    )
    weight_back = lax.all_to_all(
        weight_grad.reshape(source_count, slot_count),
        "expert",
        split_axis=0,
        concat_axis=0,
        tiled=True,
    )
    expert_out = unpack_rows(fwd_back, fwd_index, top_count).astype(jnp.float32)
    mixed_rows = fwd_rows.astype(jnp.float32) + jnp.sum(
        fwd_weights[0][:, :, None] * expert_out, axis=1
    )
    handed = from_behind(mixed_rows.astype(jnp.bfloat16), "segment", 1)
    choice_grad = unpack_rows(grad_back, bwd_index, top_count).astype(jnp.float32)
    normed_grad = jnp.sum(bwd_weights[0][:, :, None] * choice_grad, axis=1)
    scaled_grad = normed_grad * gain_row
    values = bwd_rows.astype(jnp.float32)
    inner_mean = jnp.mean(values * scaled_grad, axis=-1, keepdims=True)
    input_grad = (
        grad_rows.astype(jnp.float32)
        + saved_scale * scaled_grad
        - values * saved_scale * saved_scale * saved_scale * inner_mean
    )
    returned = from_behind(input_grad.astype(jnp.bfloat16), "segment", -1)
    combine_rows = unpack_rows(weight_back, bwd_index, top_count)
    return (handed[None], returned[None], combine_rows[None])


def solution(mesh):
    return jax.shard_map(
        body,
        mesh=mesh,
        in_specs=(
            P("segment", "expert", None),
            P("segment", "expert", None),
            P("segment", "expert", None),
            P("segment", "expert", None),
            P("segment", "expert", None),
            P("segment", "expert", None),
            P("segment", "expert", None),
            P("segment", None),
            P("segment", "expert", None, None),
            P("segment", "expert", None, None),
            P("segment", "expert", None, None),
        ),
        out_specs=(
            P("segment", "expert", None),
            P("segment", "expert", None),
            P("segment", "expert", None),
        ),
        check_vma=False,
    )
```

profile of v0, /device:TPU:1, one launch (start us, length us, event | category | flops | bytes accessed | tf_op | source)
XLA Modules:
  0.0 381.5 jit_solution(9639935250562450002)
XLA Ops:
  0.6 0.8 broadcast_multiply_fusion
  1.5 0.9 copy.34
  2.7 1.2 fusion.38
  3.9 1.2 fusion.42
  5.4 0.6 reduce-window.16
  6.2 1.2 fusion.33
  7.5 1.6 broadcast_in_dim.13
  9.1 2.3 reshape.250
  11.4 4.4 %scatter_custom_fusion.2 = bf16[512,2048]{1,0:T(8,128)(2,1)} fusion(s32[256]{0:T(256)S(1)} %bitcast.122, bf16[256,2048]{1,0:T(8,128)(2,1)} %reshape.250, bf16[]{:T(256)} %constant.8.clone.1), kind=kCustom, calls=%fused_computation.55 | custom fusion | bytes 2097664 | tf_op jit(solution)/shard_map/scatter | solution.py:30
  15.9 10.1 %all-to-all-start.3 = ((bf16[16,32,2048]{2,1,0:T(8,128)(2,1)}), bf16[16,32,2048]{2,1,0:T(8,128)(2,1)}, u32[]{:S(2)}, u32[]{:S(2)}) async-start(bf16[16,32,2048]{2,1,0:T(8,128)(2,1)} %bitcast.112), calls=%async_computation.3 | async-start | bytes 4194304 | tf_op jit(solution)/shard_map/all_to_all | solution.py:116
  26.0 2.7 broadcast_in_dim.12
  28.6 2.3 reshape.242
  30.9 4.4 %scatter_custom_fusion.1 = bf16[512,2048]{1,0:T(8,128)(2,1)} fusion(s32[256]{0:T(256)S(1)} %bitcast.123, bf16[256,2048]{1,0:T(8,128)(2,1)} %reshape.242, bf16[]{:T(256)} %constant.8.clone.1), kind=kCustom, calls=%fused_computation.57 | custom fusion | bytes 2097664 | tf_op jit(solution)/shard_map/scatter | solution.py:30
  35.3 38.4 %all-to-all-done.3 = bf16[16,32,2048]{2,1,0:T(8,128)(2,1)} async-done(((bf16[16,32,2048]{2,1,0:T(8,128)(2,1)}), bf16[16,32,2048]{2,1,0:T(8,128)(2,1)}, u32[]{:S(2)}, u32[]{:S(2)}) %all-to-all-start.3) | async-done | bytes 2097184 | tf_op jit(solution)/shard_map/all_to_all | solution.py:116
  73.7 7.4 %all-to-all-start.2 = ((bf16[16,32,2048]{2,1,0:T(8,128)(2,1)}), bf16[16,32,2048]{2,1,0:T(8,128)(2,1)}, u32[]{:S(2)}, u32[]{:S(2)}) async-start(bf16[16,32,2048]{2,1,0:T(8,128)(2,1)} %bitcast.111), calls=%async_computation.2 | async-start | bytes 4194304 | tf_op jit(solution)/shard_map/all_to_all | solution.py:117
  81.0 5.5 %fusion.14 = f32[512,768]{1,0:T(8,128)} fusion(bf16[512,2048]{1,0:T(8,128)(2,1)} %bitcast.25, bf16[1,1,2048,768]{3,2,1,0:T(8,128)(2,1)} %param.19), kind=kOutput, calls=%fused_computation.22 | convolution fusion | flops 1610612736 | bytes 6815744 | tf_op jit(solution)/shard_map/dot_general | solution.py:42
  86.6 4.5 %fusion.8 = f32[512,768]{1,0:T(8,128)} fusion(bf16[512,2048]{1,0:T(8,128)(2,1)} %bitcast.25, bf16[1,1,2048,768]{3,2,1,0:T(8,128)(2,1)S(1)} %copy-done), kind=kOutput, calls=%fused_computation.16 | convolution fusion | flops 1610612736 | bytes 6815744 | tf_op jit(solution)/shard_map/dot_general | solution.py:42
  91.1 37.7 %all-to-all-done.2 = bf16[16,32,2048]{2,1,0:T(8,128)(2,1)} async-done(((bf16[16,32,2048]{2,1,0:T(8,128)(2,1)}), bf16[16,32,2048]{2,1,0:T(8,128)(2,1)}, u32[]{:S(2)}, u32[]{:S(2)}) %all-to-all-start.2) | async-done | bytes 2097184 | tf_op jit(solution)/shard_map/all_to_all | solution.py:117
  128.8 4.5 %fusion.2 = f32[512,768]{1,0:T(8,128)S(1)} fusion(bf16[512,2048]{1,0:T(8,128)(2,1)} %bitcast.22, bf16[1,1,768,2048]{3,2,1,0:T(8,128)(2,1)} %param.21), kind=kOutput, calls=%fused_computation.10 | convolution fusion | flops 1610612736 | bytes 6815744 | tf_op jit(solution)/shard_map/dot_general | solution.py:46
  133.3 1.9 fusion.6
  135.7 3.6 add_convert_fusion
  139.3 7.5 %all-to-all-start.4 = ((bf16[16,32,2048]{2,1,0:T(8,128)(2,1)}), bf16[16,32,2048]{2,1,0:T(8,128)(2,1)}, u32[]{:S(2)}, u32[]{:S(2)}) async-start(bf16[16,32,2048]{2,1,0:T(8,128)(2,1)} %bitcast.114), calls=%async_computation.4 | async-start | bytes 4194304 | tf_op jit(solution)/shard_map/all_to_all | solution.py:136
  148.5 46.1 %all-to-all-done.4 = bf16[16,32,2048]{2,1,0:T(8,128)(2,1)} async-done(((bf16[16,32,2048]{2,1,0:T(8,128)(2,1)}), bf16[16,32,2048]{2,1,0:T(8,128)(2,1)}, u32[]{:S(2)}, u32[]{:S(2)}) %all-to-all-start.4) | async-done | bytes 2097184 | tf_op jit(solution)/shard_map/all_to_all | solution.py:136
  194.6 5.2 %gather_fusion.1 = bf16[256,2048]{1,0:T(8,128)(2,1)} fusion(bf16[512,2048]{1,0:T(8,128)(2,1)} %bitcast.27, s32[1024]{0:T(1024)S(1)} %pad_clamp_fusion), kind=kCustom, calls=%fused_computation.1 | custom fusion | bytes 2098176 | tf_op jit(solution)/shard_map/gather | solution.py:37
  199.8 3.3 reshape.205
  203.1 4.9 %multiply_reduce_fusion.1 = f32[128,2048]{1,0:T(8,128)S(1)} fusion(f32[128,2,2048]{2,1,0:T(2,128)} %reshape.205, f32[128,2]{1,0:T(8,128)S(1)} %copy.32), kind=kLoop, calls=%fused_computation.28 | loop fusion | flops 786432 | bytes 3146752 | tf_op jit(solution)/shard_map/reduce_sum | solution.py:156
  208.3 1.2 fusion.37
  209.5 1.6 broadcast_in_dim.10
  211.2 2.3 reshape.234
  213.5 4.4 %scatter_custom_fusion = bf16[512,2048]{1,0:T(8,128)(2,1)} fusion(s32[256]{0:T(256)S(1)} %bitcast.125, bf16[256,2048]{1,0:T(8,128)(2,1)} %reshape.234, bf16[]{:T(256)} %constant.8.clone.1), kind=kCustom, calls=%fused_computation.59 | custom fusion | bytes 2097664 | tf_op jit(solution)/shard_map/scatter | solution.py:30
  217.8 54.4 %all_to_all.31 = bf16[16,32,2048]{2,1,0:T(8,128)(2,1)S(1)} all-to-all(bf16[16,32,2048]{2,1,0:T(8,128)(2,1)} %bitcast.113), channel_id=1, replica_groups=mesh['segment'=16,'expert'=16] {'expert'}, dimensions={0} | all-to-all | bytes 4194304 | tf_op jit(solution)/shard_map/all_to_all | solution.py:115
  272.3 1.3 copy-done.4
  273.6 3.0 fusion.16
  276.6 8.3 %fusion.18 = bf16[512,2048]{1,0:T(8,128)(2,1)} fusion(bf16[1,1,768,2048]{3,2,1,0:T(8,128)(2,1)} %param.21, f32[512,768]{1,0:T(8,128)} %fusion.16, bf16[512,2048]{1,0:T(8,128)(2,1)} %bitcast.117, bf16[1,1,2048,768]{3,2,1,0:T(8,128)(2,1)S(1)} %copy-done), kind=kOutput, calls=%fused_computation.26 | convolution fusion | flops 3224633344 | bytes 12058624 | tf_op jit(solution)/shard_map/dot_general | solution.py:42
  284.8 6.9 %all-to-all-start.1 = ((bf16[16,32,2048]{2,1,0:T(8,128)(2,1)}), bf16[16,32,2048]{2,1,0:T(8,128)(2,1)}, u32[]{:S(2)}, u32[]{:S(2)}) async-start(bf16[16,32,2048]{2,1,0:T(8,128)(2,1)} %bitcast.115), calls=%async_computation.1 | async-start | bytes 4194304 | tf_op jit(solution)/shard_map/all_to_all | solution.py:129
  291.9 1.4 collective-permute-start.1
  293.3 45.3 %all-to-all-done.1 = bf16[16,32,2048]{2,1,0:T(8,128)(2,1)} async-done(((bf16[16,32,2048]{2,1,0:T(8,128)(2,1)}), bf16[16,32,2048]{2,1,0:T(8,128)(2,1)}, u32[]{:S(2)}, u32[]{:S(2)}) %all-to-all-start.1) | async-done | bytes 2097184 | tf_op jit(solution)/shard_map/all_to_all | solution.py:129
  338.6 5.2 %gather_fusion = bf16[256,2048]{1,0:T(8,128)(2,1)} fusion(bf16[512,2048]{1,0:T(8,128)(2,1)} %bitcast.13, s32[1024]{0:T(1024)S(1)} %pad_clamp_fusion.1), kind=kCustom, calls=%fused_computation | custom fusion | bytes 2098176 | tf_op jit(solution)/shard_map/gather | solution.py:37
  343.8 3.3 reshape.203
  347.1 5.0 %multiply_reduce_fusion.2 = f32[128,2048]{1,0:T(8,128)S(1)} fusion(f32[128,2,2048]{2,1,0:T(2,128)} %reshape.203, f32[128,2]{1,0:T(8,128)S(1)} %copy.27), kind=kLoop, calls=%fused_computation.29 | loop fusion | flops 786432 | bytes 3146752 | tf_op jit(solution)/shard_map/reduce_sum | solution.py:151
  352.1 0.9 fusion.41
  353.0 5.2 %collective-permute-start = (bf16[128,2048]{1,0:T(8,128)(2,1)}, bf16[128,2048]{1,0:T(8,128)(2,1)}, u32[]{:S(2)}, u32[]{:S(2)}) collective-permute-start(bf16[128,2048]{1,0:T(8,128)(2,1)} %fusion.41), channel_id=1, source_target_pairs={{0,16},{16,32},{32,48},{48,64},{64,80},{80,96},{96,112},{112,128},... | collective-permute-start | bytes 1572872 | tf_op jit(solution)/shard_map/ppermute | solution.py:12
  358.2 4.1 %multiply_reduce_fusion = bf16[512]{0:T(512)(128)(2,1)S(1)} fusion(bf16[512,2048]{1,0:T(8,128)(2,1)} %bitcast.22, bf16[1,1,768,2048]{3,2,1,0:T(8,128)(2,1)S(1)} %copy-done.12, f32[512,768]{1,0:T(8,128)} %fusion.8, f32[512,768]{1,0:T(8,128)S(1)} %copy-done.14), kind=kOutput, calls=%fused_computation.6 | convolution fusion | flops 1618214400 | bytes 8389632 | tf_op jit(solution)/shard_map/dot_general | solution.py:42
  362.4 12.0 %all_to_all.32 = bf16[16,1,32]{2,1,0:T(2,128)(2,1)S(1)} all-to-all(bf16[16,1,32]{2,1,0:T(2,128)(2,1)S(1)} %convert_element_type.128), channel_id=1, replica_groups=mesh['segment'=16,'expert'=16] {'expert'}, dimensions={0} | all-to-all | bytes 2048 | tf_op jit(solution)/shard_map/all_to_all | solution.py:143
  374.5 1.9 gather_fusion.2
  376.6 0.6 copy.38
  377.2 1.9 copy.45
  379.1 1.9 copy.46
  (67 shorter events, 3.8 us)
Async XLA Ops:
  0.6 86.0 %copy-start = (bf16[1,1,2048,768]{3,2,1,0:T(8,128)(2,1)S(1)}, bf16[1,1,2048,768]{3,2,1,0:T(8,128)(2,1)}, u32[]{:S(2)}) copy-start(bf16[1,1,2048,768]{3,2,1,0:T(8,128)(2,1)} %param.20) | copy-start | bytes 9437188
  15.9 57.8 %all-to-all-start.3 = ((bf16[16,32,2048]{2,1,0:T(8,128)(2,1)}), bf16[16,32,2048]{2,1,0:T(8,128)(2,1)}, u32[]{:S(2)}, u32[]{:S(2)}) async-start(bf16[16,32,2048]{2,1,0:T(8,128)(2,1)} %bitcast.112), calls=%async_computation.3 | async-start | bytes 4194304 | tf_op jit(solution)/shard_map/all_to_all | solution.py:116
  73.7 55.2 %all-to-all-start.2 = ((bf16[16,32,2048]{2,1,0:T(8,128)(2,1)}), bf16[16,32,2048]{2,1,0:T(8,128)(2,1)}, u32[]{:S(2)}, u32[]{:S(2)}) async-start(bf16[16,32,2048]{2,1,0:T(8,128)(2,1)} %bitcast.111), calls=%async_computation.2 | async-start | bytes 4194304 | tf_op jit(solution)/shard_map/all_to_all | solution.py:117
  128.8 4.5 %copy-start.13 = (f32[512,768]{1,0:T(8,128)S(1)}, f32[512,768]{1,0:T(8,128)}, u32[]{:S(2)}) copy-start(f32[512,768]{1,0:T(8,128)} %fusion.14) | copy-start | bytes 4718596
  133.3 1.9 copy-start.10
  133.3 2.3 copy-start.15
  139.3 7.5 %copy-start.7 = (s32[1,128,2]{1,2,0:T(2,128)S(1)}, s32[1,128,2]{1,2,0:T(2,128)}, u32[]{:S(2)}) copy-start(s32[1,128,2]{1,2,0:T(2,128)} %param.12) | copy-start | bytes 3076
  139.3 9.0 %copy-start.8 = (f32[1,128,2]{1,2,0:T(2,128)S(1)}, f32[1,128,2]{1,2,0:T(2,128)}, u32[]{:S(2)}) copy-start(f32[1,128,2]{1,2,0:T(2,128)} %param.16) | copy-start | bytes 3076
  139.3 55.3 %all-to-all-start.4 = ((bf16[16,32,2048]{2,1,0:T(8,128)(2,1)}), bf16[16,32,2048]{2,1,0:T(8,128)(2,1)}, u32[]{:S(2)}, u32[]{:S(2)}) async-start(bf16[16,32,2048]{2,1,0:T(8,128)(2,1)} %bitcast.114), calls=%async_computation.4 | async-start | bytes 4194304 | tf_op jit(solution)/shard_map/all_to_all | solution.py:136
  203.1 4.9 %copy-start.1 = (bf16[1,128,2048]{2,1,0:T(8,128)(2,1)S(1)}, bf16[1,128,2048]{2,1,0:T(8,128)(2,1)}, u32[]{:S(2)}) copy-start(bf16[1,128,2048]{2,1,0:T(8,128)(2,1)} %param.14) | copy-start | bytes 1572868
  203.1 5.0 %copy-start.6 = (f32[1,2048]{1,0:T(1,128)S(1)}, f32[1,2048]{1,0:T(1,128)}, u32[]{:S(2)}) copy-start(f32[1,2048]{1,0:T(1,128)} %param.18) | copy-start | bytes 24580
  203.1 5.2 %copy-start.2 = (bf16[1,128,2048]{2,1,0:T(8,128)(2,1)S(1)}, bf16[1,128,2048]{2,1,0:T(8,128)(2,1)}, u32[]{:S(2)}) copy-start(bf16[1,128,2048]{2,1,0:T(8,128)(2,1)} %param.11) | copy-start | bytes 1572868
  203.1 5.2 %copy-start.5 = (bf16[1,128,2048]{2,1,0:T(8,128)(2,1)S(1)}, bf16[1,128,2048]{2,1,0:T(8,128)(2,1)}, u32[]{:S(2)}) copy-start(bf16[1,128,2048]{2,1,0:T(8,128)(2,1)} %param.17) | copy-start | bytes 1572868
  217.8 55.8 %copy-start.11 = (bf16[1,1,2048,768]{3,2,1,0:T(8,128)(2,1)S(1)}, bf16[1,1,2048,768]{3,2,1,0:T(8,128)(2,1)}, u32[]{:S(2)}) copy-start(bf16[1,1,2048,768]{3,2,1,0:T(8,128)(2,1)} %param.19) | copy-start | bytes 9437188
  272.3 1.3 copy-start.4
  284.8 6.9 %copy-start.9 = (f32[1,128,2]{1,2,0:T(2,128)S(1)}, f32[1,128,2]{1,2,0:T(2,128)}, u32[]{:S(2)}) copy-start(f32[1,128,2]{1,2,0:T(2,128)} %param.13) | copy-start | bytes 3076
  284.8 53.7 %all-to-all-start.1 = ((bf16[16,32,2048]{2,1,0:T(8,128)(2,1)}), bf16[16,32,2048]{2,1,0:T(8,128)(2,1)}, u32[]{:S(2)}, u32[]{:S(2)}) async-start(bf16[16,32,2048]{2,1,0:T(8,128)(2,1)} %bitcast.115), calls=%async_computation.1 | async-start | bytes 4194304 | tf_op jit(solution)/shard_map/all_to_all | solution.py:129
  291.9 85.4 %collective-permute-start.1 = (bf16[128,2048]{1,0:T(8,128)(2,1)}, bf16[128,2048]{1,0:T(8,128)(2,1)}, u32[]{:S(2)}, u32[]{:S(2)}) collective-permute-start(bf16[128,2048]{1,0:T(8,128)(2,1)} %get-tuple-element.9), channel_id=1, source_target_pairs={{0,240},{16,0},{32,16},{48,32},{64,48},{80,64},{96,80},{112,96},{1... | collective-permute-start | bytes 1572872 | tf_op jit(solution)/shard_map/ppermute | solution.py:12
  347.1 5.0 %copy-start.3 = (bf16[1,128,2048]{2,1,0:T(8,128)(2,1)S(1)}, bf16[1,128,2048]{2,1,0:T(8,128)(2,1)}, u32[]{:S(2)}) copy-start(bf16[1,128,2048]{2,1,0:T(8,128)(2,1)} %param.11) | copy-start | bytes 1572868
  347.1 11.1 %copy-start.12 = (bf16[1,1,768,2048]{3,2,1,0:T(8,128)(2,1)S(1)}, bf16[1,1,768,2048]{3,2,1,0:T(8,128)(2,1)}, u32[]{:S(2)}) copy-start(bf16[1,1,768,2048]{3,2,1,0:T(8,128)(2,1)} %param.21) | copy-start | bytes 9437188
  347.1 11.1 %copy-start.14 = (f32[512,768]{1,0:T(8,128)S(1)}, f32[512,768]{1,0:T(8,128)}, u32[]{:S(2)}) copy-start(f32[512,768]{1,0:T(8,128)} %fusion.14) | copy-start | bytes 4718596
  353.0 24.2 %collective-permute-start = (bf16[128,2048]{1,0:T(8,128)(2,1)}, bf16[128,2048]{1,0:T(8,128)(2,1)}, u32[]{:S(2)}, u32[]{:S(2)}) collective-permute-start(bf16[128,2048]{1,0:T(8,128)(2,1)} %fusion.41), channel_id=1, source_target_pairs={{0,16},{16,32},{32,48},{48,64},{64,80},{80,96},{96,112},{112,128},... | collective-permute-start | bytes 1572872 | tf_op jit(solution)/shard_map/ppermute | solution.py:12
where the time goes:
time: 389 us; the launch traced here: 382 us
  waiting for transfers between devices  167 us (43%)
  blocking collectives  66.4 us (17%)
  local copies, waits for them, and re-layouts  54.1 us (14%)
  starting transfers between devices  38.5 us (10%)
  matrix products  35.3 us (9%)
  other arithmetic  18.3 us (5%)
    all_to_all x1, blocking collectives, body(): lax.all_to_all(fwd_send, 'expert', split_axis=0, concat_axis=0, tiled=True)  54.4 us
    all_to_all x1, waiting for transfers between devices, body(): lax.all_to_all(row_grad.reshape(source_count, slot_count, feature_width),...  46.1 us
    all_to_all x1, waiting for transfers between devices, body(): lax.all_to_all(fwd_out.reshape(source_count, slot_count, feature_width),...  45.3 us
    all_to_all x1, waiting for transfers between devices, body(): lax.all_to_all(saved_send, 'expert', split_axis=0, concat_axis=0, tiled=T...  38.4 us
    all_to_all x1, waiting for transfers between devices, body(): lax.all_to_all(grad_send, 'expert', split_axis=0, concat_axis=0, tiled=True)  37.7 us
    dot_general x5, matrix products, dot_rows(): return jnp.dot(left_rows, right_matrix, preferred_element_type=jnp.float32)  25.3 us
    scatter x3, local copies, waits for them, and re-layouts, pack_rows(): packed = jnp.zeros((expert_count * capacity, token_rows.shape[1]), token_...  13.2 us
    gather x3, local copies, waits for them, and re-layouts, unpack_rows(): picked = flat_rows[slot_rows]  12.3 us
  transfers between devices with their start and end apart: 6, of which 4 were waited for; matrix products, arithmetic and copies ran while one was open for 11% of the time, Pallas kernels for 0%

commit v1 on v0

v1 whole, which is shorter than its diff:
```python
import functools

import jax
import jax.numpy as jnp
from jax import lax
from jax.experimental import pallas as pl
from jax.experimental.pallas import tpu as pltpu
from jax.sharding import PartitionSpec as P

EPS = 1e-06
MESH = pl.DeviceIdType.MESH
F32 = jnp.float32
BF16 = jnp.bfloat16
SLOTS = 32
TOK = 128
RING = 8
REACH = (TOK, TOK, 3 * SLOTS, SLOTS)
SAVED, GRAD, FWD = 0, 1, 2
BWD_ROUTE, FWD_ROUTE = 0, 1
LAST = 7


def block_of(way, hop):
    return LAST if hop == 4 else 3 * way + hop


def iota(shape, dim):
    return lax.broadcasted_iota(jnp.int32, shape, dim)


def dot(a, b):
    return jnp.dot(a, b, preferred_element_type=F32)


def dot_t(a, b):
    return lax.dot_general(a, b, (((1,), (1,)), ((), ())), preferred_element_type=F32)


def hops_of(route, z, x):
    offset = jnp.bitwise_and(route - z + RING, RING - 1)
    other = jnp.where(jnp.right_shift(route, 3) != x, 1, 0)
    half = offset == RING // 2
    plus = jnp.where(offset < RING // 2, offset, jnp.where(half & (other == 0), RING // 2, 0))
    minus = jnp.where(offset > RING // 2, RING - offset, jnp.where(half & (other == 1), RING // 2, 0))
    return (plus, minus), other, offset


def code_of(hop, other):
    return jnp.where(hop > 0, 2 * (hop - 1) + other, -1)


def selector(meta, row):
    slot = iota((SLOTS, TOK), 0).astype(F32) + 1.0
    own = jnp.where(slot == meta[row : row + 1, :], 1.0, 0.0)
    other = jnp.where(slot == meta[row + 1 : row + 2, :], 1.0, 0.0)
    return own, other


def spreader(meta, row):
    own, other = selector(meta, row)
    w_own, w_other = meta[row + 2 : row + 3, :], meta[row + 3 : row + 4, :]
    hi_own, hi_other = w_own.astype(BF16).astype(F32), w_other.astype(BF16).astype(F32)
    stacked = jnp.concatenate(
        [own * hi_own, other * hi_other, own * (w_own - hi_own), other * (w_other - hi_other)], axis=0
    )
    return jnp.transpose(stacked).astype(BF16)


def kernel(
    tokens_f, routes_f, weights_f, tokens_b, routes_b, weights_b, grads, gain, gate_hbm, up_hbm, down_hbm,
    next_input, next_grad, combine,
    packed, r1, r2, r3, r4, meta0, meta1, meta2, meta3, meta4, meta_here, back,
    xsend, xin, w_gate, w_up, w_down, hid_a, hid_b, y_b, y_f, yx_b, yx_f,
    t1, t2, t3, t4, ct_out, ct_in, res, done_f, done_b,
    d_send, d_recv, m_send, m_recv, x_send, x_recv, y_send, y_recv, t_send, t_recv, c_send, c_recv, s_send, s_recv, w_sem,
):
    me = lax.axis_index("expert")
    z, x = lax.rem(me, RING), me // RING
    seg = lax.axis_index("segment")
    sections = lax.axis_size("segment")
    ahead = {"expert": x * RING + lax.rem(z + 1, RING)}
    behind = {"expert": x * RING + lax.rem(z + RING - 1, RING)}
    across = {"expert": (1 - x) * RING + z}
    seg_next = {"segment": lax.rem(seg + 1, sections)}
    seg_prev = {"segment": lax.rem(seg + sections - 1, sections)}
    onward, homeward = (ahead, behind), (behind, ahead)
    width = tokens_f.shape[1]
    hidden = w_gate.shape[1]
    tile = 512
    tiles = width // tile

    loads = [
        pltpu.make_async_copy(src, dst, w_sem.at[i])
        for i, (src, dst) in enumerate(((gate_hbm, w_gate), (up_hbm, w_up), (down_hbm, w_down)))
    ]
    for load in loads:
        load.start()
    barrier = pltpu.get_barrier_semaphore()
    for device in (ahead, behind, across, seg_next, seg_prev):
        pl.semaphore_signal(barrier, inc=1, device_id=device, device_id_type=MESH)

    def over_tiles(body, size=tile):
        @pl.loop(0, width // size)
        def _(i):
            body(pl.ds(pl.multiple_of(i * size, size), size))

    landing = {1: r1, 2: r2, 3: r3}
    returning = {1: t1, 2: t2, 3: t3}
    metas = (meta0, meta1, meta2, meta3, meta4)

    def landed(array, way, hop):
        if hop == 4:
            return r4.at[array, pl.ds(way * SLOTS, SLOTS)]
        return landing[hop].at[array, way]

    def returned(array, way, hop):
        if hop == 4:
            return t4.at[array, pl.ds(way * SLOTS, SLOTS)]
        return returning[hop].at[array, way]

    def remote(src, dst, send, recv, device):
        return pltpu.make_async_remote_copy(
            src_ref=src, dst_ref=dst, send_sem=send, recv_sem=recv, device_id=device, device_id_type=MESH
        )

    def dispatch(array, way, hop):
        source = packed.at[array, way] if hop == 1 else landing[hop - 1].at[array, way]
        rows = REACH[hop - 1]
        at = (array, way, hop - 1)
        return remote(
            source.at[pl.ds(0, rows)], landed(array, way, hop), d_send.at[at], d_recv.at[at], onward[way]
        )

    def meta_copy(route, way, hop):
        at = (route, way, hop - 1)
        return remote(
            metas[hop - 1].at[route, way], metas[hop].at[route, way], m_send.at[at], m_recv.at[at], onward[way]
        )

    def cross(array, block):
        here = pl.ds(block * SLOTS, SLOTS)
        there = pl.ds((8 + block) * SLOTS, SLOTS)
        at = (array, block)
        return remote(xsend.at[array, here], xin.at[array, there], x_send.at[at], x_recv.at[at], across)

    outs, outs_x = (y_b, y_f), (yx_b, yx_f)

    def cross_back(which, block):
        there = pl.ds(block * SLOTS, SLOTS)
        here = pl.ds((8 + block) * SLOTS, SLOTS)
        at = (which, block)
        return remote(
            outs[which].at[here], outs_x[which].at[there], y_send.at[at], y_recv.at[at], across
        )

    reused = (SAVED, FWD)

    def give_back(which, way, hop):
        at = (which, way, hop - 1)
        return remote(
            landed(reused[which], way, hop), returned(which, way, hop), t_send.at[at], t_recv.at[at], homeward[way]
        )

    def give_scalars(way, hop):
        at = (way, hop - 1)
        return remote(ct_out.at[at], ct_in.at[at], c_send.at[at], c_recv.at[at], homeward[way])

    lane = iota((TOK, TOK), 1)
    sub = iota((TOK, TOK), 0)

    def plan(route, routes_ref, weights_ref):
        r_col = [routes_ref[:, k : k + 1] for k in range(2)]
        w_col = [weights_ref[:, k : k + 1] for k in range(2)]
        columns = jnp.zeros((TOK, TOK), F32)
        for j, col in enumerate([r_col[0].astype(F32), r_col[1].astype(F32), w_col[0], w_col[1]]):
            columns = jnp.where(lane == j, col, columns)
        across_rows = jnp.transpose(columns)
        r_row = [across_rows[k : k + 1, :].astype(jnp.int32) for k in range(2)]
        w_row = [across_rows[2 + k : 3 + k, :] for k in range(2)]
        slot_row = []
        for k in range(2):
            earlier = jnp.where((sub < lane) & ((r_col[0] == r_row[k]) | (r_col[1] == r_row[k])), 1.0, 0.0)
            slot_row.append(jnp.sum(earlier, axis=0, keepdims=True) + 1.0)
        info_col = [hops_of(r, z, x) for r in r_col]
        info_row = [hops_of(r, z, x) for r in r_row]
        kind = iota((8, TOK), 0)
        here = jnp.zeros((8, TOK), F32)
        for k in range(2):
            _, other, offset = info_row[k]
            value = jnp.where(kind < 2, slot_row[k], w_row[k])
            here = here + jnp.where((offset == 0) & (jnp.bitwise_and(kind, 1) == other) & (kind < 4), value, 0.0)
        meta_here[route] = here
        j = iota((16, TOK), 0)
        target = 2 * jnp.right_shift(j, 2) + jnp.bitwise_and(j, 1)
        is_slot = jnp.bitwise_and(j, 2) == 0
        orders = []
        for way in range(2):
            far_col = jnp.maximum(info_col[0][0][way], info_col[1][0][way])
            far_row = jnp.maximum(info_row[0][0][way], info_row[1][0][way])
            ahead_of_row = (far_col > far_row) | ((far_col == far_row) & (sub < lane))
            pos_row = jnp.sum(jnp.where(ahead_of_row, 1.0, 0.0), axis=0, keepdims=True)
            ahead_of_col = (far_row > far_col) | ((far_row == far_col) & (lane < sub))
            pos_col = jnp.sum(jnp.where(ahead_of_col, 1.0, 0.0), axis=1, keepdims=True)
            order = jnp.where(sub.astype(F32) == pos_row, 1.0, 0.0).astype(BF16)
            back[route, way] = jnp.where(lane.astype(F32) == pos_col, 1.0, 0.0).astype(BF16)
            meta = jnp.zeros((16, TOK), F32)
            for k in range(2):
                code = code_of(info_row[k][0][way], info_row[k][1])
                meta = meta + jnp.where(code == target, jnp.where(is_slot, slot_row[k], w_row[k]), 0.0)
            high = meta.astype(BF16)
            low = (meta - high.astype(F32)).astype(BF16)
            meta0[route, way] = dot_t(high, order) + dot_t(low, order)
            orders.append(order)
        return orders

    def scale_of(tokens):
        values = tokens[...].astype(F32)
        return lax.rsqrt(jnp.mean(values * values, axis=-1, keepdims=True) + EPS)

    def normalize(tokens, out):
        inv = scale_of(tokens)

        def body(cols):
            out[:, cols] = (tokens[:, cols].astype(F32) * inv * gain[:, cols]).astype(BF16)

        over_tiles(body)

    def pack(array, way, order, rows):
        def body(cols):
            packed[array, way, :, cols] = dot(order, rows[:, cols]).astype(BF16)

        over_tiles(body)

    def pick_here(array, route, rows):
        own, other = selector(meta_here.at[route], 0)
        both = jnp.concatenate([own, other], axis=0).astype(BF16)

        def body(cols):
            picked = dot(both, rows[:, cols]).astype(BF16)
            xin[array, 0:SLOTS, cols] = picked[:SLOTS]
            xsend[array, 0:SLOTS, cols] = picked[SLOTS:]

        over_tiles(body)
        cross(array, 0).start()

    def pick(array, route, ways, hop):
        block = block_of(ways[0], hop)
        rows = REACH[hop - 1]
        at = pl.ds(block * SLOTS, SLOTS)
        matrices = []
        for way in ways:
            own, other = selector(metas[hop].at[route, way], 4 * (hop - 1))
            matrices.append(jnp.concatenate([own, other], axis=0)[:, :rows].astype(BF16))

        def body(cols):
            picked = sum(dot(m, landed(array, w, hop)[:, cols]) for m, w in zip(matrices, ways)).astype(BF16)
            xin[array, at, cols] = picked[:SLOTS]
            xsend[array, at, cols] = picked[SLOTS:]

        over_tiles(body)
        cross(array, block).start()

    def advance(array, hop, route=None):
        for way in range(2):
            if route is not None:
                meta_copy(route, way, hop).wait_recv()
                if hop < 4:
                    meta_copy(route, way, hop + 1).start()
            dispatch(array, way, hop).wait_recv()
            if hop < 4:
                dispatch(array, way, hop + 1).start()

    def pick_all(array, hop, route):
        if hop == 4:
            pick(array, route, (0, 1), 4)
        else:
            pick(array, route, (0,), hop)
            pick(array, route, (1,), hop)

    def spread(which, route, way, hop):
        rows = REACH[hop - 1]
        further = REACH[hop] if hop < 4 else 0
        block = block_of(way, hop)
        at = pl.ds(block * SLOTS, SLOTS)
        meta = metas[hop].at[route, way]
        matrix = spreader(meta, 4 * (hop - 1))[:rows]
        if hop < 4:
            give_back(which, way, hop + 1).wait_recv()
        target = landed(reused[which], way, hop)

        def body(cols):
            own, other = outs[which][at, cols], outs_x[which][at, cols]
            total = dot(matrix, jnp.concatenate([own, other, own, other], axis=0))
            if further:
                came = returned(which, way, hop + 1)[:, cols].astype(F32)
                if further < rows:
                    came = jnp.concatenate([came, jnp.zeros((rows - further, tile), F32)], axis=0)
                total = total + came
            target[:, cols] = total.astype(BF16)

        over_tiles(body)
        give_back(which, way, hop).start()
        if which == 0:
            extra = pl.ds(width, TOK)
            own, other = selector(meta, 4 * (hop - 1))
            scalars = scalar_rows(own, other, y_b[at, extra], yx_b[at, extra], hop)
            if hop < 4:
                give_scalars(way, hop + 1).wait_recv()
                scalars = scalars + ct_in[way, hop]
            ct_out[way, hop - 1] = scalars
            give_scalars(way, hop).start()

    def scalar_rows(own, other, mine, theirs, hop):
        row = iota((8, TOK), 0)
        first = jnp.sum(own * mine.astype(F32), axis=0, keepdims=True)
        second = jnp.sum(other * theirs.astype(F32), axis=0, keepdims=True)
        return jnp.where(row == 2 * (hop - 1), first, jnp.where(row == 2 * (hop - 1) + 1, second, 0.0))

    def gather_sums(which, route):
        matrix = spreader(meta_here.at[route], 0)
        orders = [back[route, way][:, : REACH[0]] for way in range(2)]
        at = pl.ds(0, SLOTS)
        for way in range(2):
            give_back(which, way, 1).wait_recv()

        def body(cols):
            own, other = outs[which][at, cols], outs_x[which][at, cols]
            total = dot(matrix, jnp.concatenate([own, other, own, other], axis=0))
            for way in range(2):
                total = total + dot(orders[way], returned(which, way, 1)[:, cols])
            res[:, cols] = total

        over_tiles(body)

    def backward_hidden():
        @pl.loop(0, hidden // 256)
        def _(i):
            cols = pl.ds(pl.multiple_of(i * 256, 256), 256)
            gate = dot(xin[SAVED], w_gate[:, cols])
            up = dot(xin[SAVED], w_up[:, cols])
            back_in = dot_t(xin[GRAD], w_down[cols, :])
            sigmoid = jax.nn.sigmoid(gate)
            active = gate * sigmoid
            rounded = (active * up).astype(BF16).astype(F32)
            part = jnp.sum(rounded * back_in, axis=1, keepdims=True)
            hid_a[:, cols] = (back_in * up * sigmoid * (1.0 + gate * (1.0 - sigmoid))).astype(BF16)
            hid_b[:, cols] = (back_in * active).astype(BF16)
            res_part = jnp.broadcast_to(part, (part.shape[0], TOK))

            @pl.when(i == 0)
            def _():
                done_b[...] = res_part

            @pl.when(i > 0)
            def _():
                done_b[...] = done_b[...] + res_part

        y_b[:, width : width + TOK] = done_b[...].astype(BF16)

    def backward_rows():
        def body(cols):
            y_b[:, cols] = (dot_t(hid_a[...], w_gate[cols, :]) + dot_t(hid_b[...], w_up[cols, :])).astype(BF16)

        over_tiles(body)

    def forward_hidden():
        @pl.loop(0, hidden // 256)
        def _(i):
            cols = pl.ds(pl.multiple_of(i * 256, 256), 256)
            gate = dot(xin[FWD], w_gate[:, cols])
            up = dot(xin[FWD], w_up[:, cols])
            hid_a[:, cols] = (gate * jax.nn.sigmoid(gate) * up).astype(BF16)

    def forward_rows():
        def body(cols):
            y_f[:, cols] = dot(hid_a[...], w_down[:, cols]).astype(BF16)

        over_tiles(body)

    back_order = (LAST, 3, 6, 2, 5, 1, 4, 0)

    def start_cross_back(which):
        for block in back_order:
            cross_back(which, block).start()

    def wait_cross_back(which, blocks):
        for block in blocks:
            cross_back(which, block).wait_recv()

    orders_b = plan(BWD_ROUTE, routes_b, weights_b)
    normalize(tokens_b, done_f)
    pl.semaphore_wait(barrier, 5)
    for way in range(2):
        meta_copy(BWD_ROUTE, way, 1).start()
    for way in range(2):
        pack(SAVED, way, orders_b[way], done_f)
        dispatch(SAVED, way, 1).start()
    for way in range(2):
        pack(GRAD, way, orders_b[way], grads)
        dispatch(GRAD, way, 1).start()
    pick_here(SAVED, BWD_ROUTE, done_f)
    pick_here(GRAD, BWD_ROUTE, grads)
    orders_f = plan(FWD_ROUTE, routes_f, weights_f)
    normalize(tokens_f, done_f)
    for way in range(2):
        meta_copy(FWD_ROUTE, way, 1).start()
        pack(FWD, way, orders_f[way], done_f)
    pick_here(FWD, FWD_ROUTE, done_f)

    for hop in range(1, 5):
        advance(SAVED, hop, BWD_ROUTE)
        pick_all(SAVED, hop, BWD_ROUTE)
        advance(GRAD, hop)
        if hop == 3:
            for way in range(2):
                dispatch(FWD, way, 1).start()
        pick_all(GRAD, hop, BWD_ROUTE)

    for load in loads:
        load.wait()
    for block in range(8):
        cross(SAVED, block).wait_recv()
        cross(GRAD, block).wait_recv()
    backward_hidden()
    advance(FWD, 1, FWD_ROUTE)
    backward_rows()
    start_cross_back(0)
    for hop in range(1, 5):
        for way in range(2):
            dispatch(SAVED, way, hop).wait_send()
    advance(FWD, 2, FWD_ROUTE)
    wait_cross_back(0, (LAST,))
    for way in range(2):
        spread(0, BWD_ROUTE, way, 4)
    pick_all(FWD, 1, FWD_ROUTE)
    pick_all(FWD, 2, FWD_ROUTE)
    advance(FWD, 3, FWD_ROUTE)
    wait_cross_back(0, (3, 6))
    for way in range(2):
        spread(0, BWD_ROUTE, way, 3)
    pick_all(FWD, 3, FWD_ROUTE)
    advance(FWD, 4, FWD_ROUTE)
    pick_all(FWD, 4, FWD_ROUTE)
    wait_cross_back(0, (2, 5))
    for way in range(2):
        spread(0, BWD_ROUTE, way, 2)
    for block in range(8):
        cross(FWD, block).wait_recv()
    forward_hidden()
    forward_rows()
    start_cross_back(1)
    for hop in range(1, 5):
        for way in range(2):
            dispatch(FWD, way, hop).wait_send()
    wait_cross_back(0, (1, 4, 0))
    wait_cross_back(1, (LAST,))
    for way in range(2):
        spread(1, FWD_ROUTE, way, 4)
    for way in range(2):
        spread(0, BWD_ROUTE, way, 1)
    wait_cross_back(1, (3, 6))
    for way in range(2):
        spread(1, FWD_ROUTE, way, 3)

    def finish_backward():
        gather_sums(0, BWD_ROUTE)
        inv = scale_of(tokens_b)
        scaled = res[...] * gain[...]
        inner = jnp.mean(tokens_b[...].astype(F32) * scaled, axis=-1, keepdims=True)
        cubed = inv * inv * inv * inner

        def body(cols):
            values = tokens_b[:, cols].astype(F32)
            grad = grads[:, cols].astype(F32) + inv * (res[:, cols] * gain[:, cols]) - values * cubed
            packed[0, 0, :, cols] = grad.astype(BF16)

        for way in range(2):
            dispatch(GRAD, way, 1).wait_send()
        over_tiles(body)

    grad_out = remote(packed.at[0, 0], next_grad, s_send.at[0], s_recv.at[0], seg_prev)
    input_out = remote(packed.at[0, 1], next_input, s_send.at[1], s_recv.at[1], seg_next)
    finish_backward()
    grad_out.start()

    wait_cross_back(1, (2, 5))
    for way in range(2):
        spread(1, FWD_ROUTE, way, 2)

    own, other = selector(meta_here.at[BWD_ROUTE], 0)
    at = pl.ds(0, SLOTS)
    extra = pl.ds(width, TOK)
    local = scalar_rows(own, other, y_b[at, extra], yx_b[at, extra], 1)
    unit = jnp.where(lane == sub, 1.0, 0.0).astype(BF16)
    values = [dot_t(unit, local.astype(BF16))]
    for way in range(2):
        give_scalars(way, 1).wait_recv()
        values.append(dot_t(back[BWD_ROUTE, way], ct_in[way, 0].astype(BF16)))
    column = iota((TOK, 8), 1)
    picked = []
    for k in range(2):
        hops, off_column, offset = hops_of(routes_b[:, k : k + 1], z, x)
        codes = [jnp.where(offset == 0, off_column, -1)] + [code_of(hop, off_column) for hop in hops]
        total = sum(jnp.where(code == column, value, 0.0) for code, value in zip(codes, values))
        picked.append(jnp.sum(total, axis=1, keepdims=True))
    combine[...] = jnp.concatenate(picked, axis=1).astype(BF16)

    wait_cross_back(1, (1, 4, 0))
    for way in range(2):
        spread(1, FWD_ROUTE, way, 1)
    gather_sums(1, FWD_ROUTE)

    def body(cols):
        packed[0, 1, :, cols] = (tokens_f[:, cols].astype(F32) + res[:, cols]).astype(BF16)

    over_tiles(body)
    input_out.start()

    for hop in range(1, 5):
        for way in range(2):
            if hop > 1:
                dispatch(GRAD, way, hop).wait_send()
            for route in range(2):
                meta_copy(route, way, hop).wait_send()
                give_back(route, way, hop).wait_send()
            give_scalars(way, hop).wait_send()
    for block in range(8):
        for array in range(3):
            cross(array, block).wait_send()
        for which in range(2):
            cross_back(which, block).wait_send()
    for out in (grad_out, input_out):
        out.wait_send()
        out.wait_recv()


def step(
    fwd_tokens, fwd_routes, fwd_weights, saved_tokens, bwd_routes, bwd_weights, incoming_grad, norm_gain,
    gate_proj, up_proj, down_proj,
):
    rows, width = fwd_tokens.shape[1:]
    hidden = gate_proj.shape[3]
    c1, c2, c3, c4 = REACH
    every = 16 * SLOTS
    vmem = pl.BlockSpec(memory_space=pltpu.VMEM)
    hbm = pl.BlockSpec(memory_space=pl.ANY)
    dma = pltpu.SemaphoreType.DMA
    meta = pltpu.VMEM((2, 2, 16, TOK), F32)
    outs = pl.pallas_call(
        kernel,
        out_shape=(
            jax.ShapeDtypeStruct((rows, width), BF16),
            jax.ShapeDtypeStruct((rows, width), BF16),
            jax.ShapeDtypeStruct((rows, 2), BF16),
        ),
        in_specs=[vmem] * 8 + [hbm] * 3,
        out_specs=(vmem, vmem, vmem),
        scratch_shapes=[
            pltpu.VMEM((3, 2, rows, width), BF16),
            pltpu.VMEM((3, 2, c1, width), BF16),
            pltpu.VMEM((3, 2, c2, width), BF16),
            pltpu.VMEM((3, 2, c3, width), BF16),
            pltpu.VMEM((3, 2 * c4, width), BF16),
            meta, meta, meta, meta, meta,
            pltpu.VMEM((2, 8, TOK), F32),
            pltpu.VMEM((2, 2, TOK, TOK), BF16),
            pltpu.VMEM((3, every // 2, width), BF16),
            pltpu.VMEM((3, every, width), BF16),
            pltpu.VMEM((width, hidden), BF16),
            pltpu.VMEM((width, hidden), BF16),
            pltpu.VMEM((hidden, width), BF16),
            pltpu.VMEM((every, hidden), BF16),
            pltpu.VMEM((every, hidden), BF16),
            pltpu.VMEM((every, width + TOK), BF16),
            pltpu.VMEM((every, width), BF16),
            pltpu.VMEM((every // 2, width + TOK), BF16),
            pltpu.VMEM((every // 2, width), BF16),
            pltpu.VMEM((2, 2, c1, width), BF16),
            pltpu.VMEM((2, 2, c2, width), BF16),
            pltpu.VMEM((2, 2, c3, width), BF16),
            pltpu.VMEM((2, 2 * c4, width), BF16),
            pltpu.VMEM((2, 4, 8, TOK), F32),
            pltpu.VMEM((2, 4, 8, TOK), F32),
            pltpu.VMEM((rows, width), F32),
            pltpu.VMEM((rows, width), BF16),
            pltpu.VMEM((every, TOK), F32),
            dma((3, 2, 4)), dma((3, 2, 4)),
            dma((2, 2, 4)), dma((2, 2, 4)),
            dma((3, 8)), dma((3, 8)),
            dma((2, 8)), dma((2, 8)),
            dma((2, 2, 4)), dma((2, 2, 4)),
            dma((2, 4)), dma((2, 4)),
            dma((2,)), dma((2,)),
            dma((3,)),
        ],
        compiler_params=pltpu.CompilerParams(
            collective_id=0, has_side_effects=True, vmem_limit_bytes=60 * 1024 * 1024
        ),
        cost_estimate=pl.CostEstimate(
            flops=2 * every * width * hidden * 8, bytes_accessed=6 * width * hidden, transcendentals=2 * every * hidden
        ),
    )(
        fwd_tokens[0], fwd_routes[0], fwd_weights[0], saved_tokens[0], bwd_routes[0], bwd_weights[0],
        incoming_grad[0], norm_gain, gate_proj[0, 0], up_proj[0, 0], down_proj[0, 0],
    )
    return tuple(out[None] for out in outs)


def solution(mesh):
    rows = P("segment", "expert", None)
    return jax.shard_map(
        step,
        mesh=mesh,
        in_specs=(rows,) * 7 + (P("segment", None),) + (P("segment", "expert", None, None),) * 3,
        out_specs=(rows, rows, rows),
        check_vma=False,
    )
```

time: 389 us -> 226 us (0.58)
  the two profiles are of different devices: /device:TPU:1 before, /device:TPU:6 now
where the time goes in v1:
time: 226 us; the launch traced here: 225 us
  Pallas kernels  214 us (95%)
  local copies, waits for them, and re-layouts  10.8 us (5%)
    pallas_call x1, Pallas kernels, step(): pl.pallas_call(kernel, out_shape=(jax.ShapeDtypeStruct((rows, width), BF1...  214 us
    unnamed x7, local copies, waits for them, and re-layouts  10.8 us

profile of v1, /device:TPU:6, one launch (start us, length us, event | category | flops | bytes accessed | tf_op | source)
XLA Modules:
  0.0 225.2 jit_solution(261207807731243839)
XLA Ops:
  0.6 1.4 copy.14
  2.0 1.4 copy.15
  3.5 1.4 copy.16
  4.9 1.4 copy.17
  6.3 213.8 %shard_map.130 = (bf16[128,2048]{1,0:T(8,128)(2,1)}, bf16[128,2048]{1,0:T(8,128)(2,1)}, bf16[128,2]{1,0:T(8,128)(2,1)}) custom-call(bf16[128,2048]{1,0:T(8,128)(2,1)} %bitcast.23, s32[128,2]{1,0:T(8,128)} %bitcast.15, f32[128,2]{1,0:T(8,128)} %bitcast.16, bf16[128,2048]{1,0:T(8,128)(2,1)} %bitcast.24, s32[128,2]{1,0:T(8,128)} %bitcast.17, ...), custom_call_target="tpu_custom_call" | custom-call | flops 12884901888 | bytes 9437184 | tf_op jit(solution)/shard_map/pallas_call | solution.py:549
  220.1 1.4 copy.18
  221.4 1.9 copy.21
  223.3 1.9 copy.22
